TPU v7x, 128 devices: a whole 4x4x4 slice. The times are simulated.
128 devices in a mesh: dp: 2 (over z_hi), blk: 8 (over y, z_lo), seq: 8 (over x, core).
Axes of the slice: x: 4, y: 4, z: 4 (z_hi: 2, z_lo: 2; z = z_hi * 2 + z_lo), core: 2. Of those that a mesh axis runs over, the one named last changes fastest.
Arguments:
- inputs: bfloat16 [16384, 1024], P(('dp', 'blk', 'seq')), may hold values from -6 to 6
- cotangent: bfloat16 [16384, 1024], P(('dp', 'blk', 'seq')), may hold values from -6 to 6
- joint_weight: float32 [1024, 3072], P(('dp', 'seq')), may hold values from -0.1875 to 0.1875
- joint_first: float32 [1024, 3072], P(('dp', 'seq'))
- joint_second: float32 [1024, 3072], P(('dp', 'seq')), as said below
- dense_weight: float32 [1024, 1024], P(('dp', 'seq')), may hold values from -3.5 to 3.5
- dense_first: float32 [1024, 1024], P(('dp', 'seq'))
- dense_second: float32 [1024, 1024], P(('dp', 'seq')), as said below
- expand_weight: float32 [1024, 4096], P(('dp', 'seq')), may hold values from -0.1875 to 0.1875
- expand_first: float32 [1024, 4096], P(('dp', 'seq'))
- expand_second: float32 [1024, 4096], P(('dp', 'seq')), as said below
- shrink_weight: float32 [4096, 1024], P(('dp', 'seq')), may hold values from -0.09375 to 0.09375
- shrink_first: float32 [4096, 1024], P(('dp', 'seq'))
- shrink_second: float32 [4096, 1024], P(('dp', 'seq')), as said below
- vectors: float32 [1024, 13], P(('dp', 'seq')), as said below
- vectors_first: float32 [1024, 13], P(('dp', 'seq'))
- vectors_second: float32 [1024, 13], P(('dp', 'seq')), as said below
Outputs:
- output: bfloat16 [16384, 1024], P(('dp', 'blk', 'seq'))
- input_grad: float32 [16384, 1024], P(('dp', 'blk', 'seq'))
- joint_first_new: float32 [1024, 3072], P(('dp', 'seq'))
- joint_second_new: float32 [1024, 3072], P(('dp', 'seq'))
- joint_weight_new: float32 [1024, 3072], P(('dp', 'seq'))
- dense_first_new: float32 [1024, 1024], P(('dp', 'seq'))
- dense_second_new: float32 [1024, 1024], P(('dp', 'seq'))
- dense_weight_new: float32 [1024, 1024], P(('dp', 'seq'))
- expand_first_new: float32 [1024, 4096], P(('dp', 'seq'))
- expand_second_new: float32 [1024, 4096], P(('dp', 'seq'))
- expand_weight_new: float32 [1024, 4096], P(('dp', 'seq'))
- shrink_first_new: float32 [4096, 1024], P(('dp', 'seq'))
- shrink_second_new: float32 [4096, 1024], P(('dp', 'seq'))
- shrink_weight_new: float32 [4096, 1024], P(('dp', 'seq'))
- vectors_first_new: float32 [1024, 13], P(('dp', 'seq'))
- vectors_second_new: float32 [1024, 13], P(('dp', 'seq'))
- vectors_new: float32 [1024, 13], P(('dp', 'seq'))
Inputs may be any that keep to these rules, and one draw needn't show every extreme that they name: `vectors`: gains of the two norms lie in [0.7, 1.3], biases in [-0.8, 0.8]. `joint_second`: positive. `dense_second`: positive. `expand_second`: positive. `shrink_second`: positive. `vectors_second`: positive.
All inputs are finite; a program needn't handle non-finite values.
Results may differ from a plain program's by a relative error of at most 0.028.
Values may be sent and summed in bfloat16 or wider, within the bound.
A program may use at most 192 MiB of HBM per device.

v0:
```python
from functools import partial
import math

import jax
import jax.numpy as jnp
from jax import lax
from jax.sharding import PartitionSpec as P

D = 1024
HEADS = 16
HEAD_DIM = 64
ROT = 16
FF = 4096
STEP = 10


eps_norm = 1e-05
beta_one = 0.9
beta_two = 0.95
adam_eps = 1e-08
weight_decay = 0.01
masked_score = -1e30


def layer_norm(inputs, gain_vec, shift_vec):
    mean_value = jnp.mean(inputs, axis=-1, keepdims=True)
    centred = inputs - mean_value
    inv_std = lax.rsqrt(jnp.mean(centred * centred, axis=-1, keepdims=True) + eps_norm)
    normed = centred * inv_std
    return (normed * gain_vec + shift_vec, normed, inv_std)


def norm_back(grad_out, gain_vec, normed, inv_std):
    grad_normed = grad_out * gain_vec
    grad_in = inv_std * (
        grad_normed
        - jnp.mean(grad_normed, axis=-1, keepdims=True)
        - normed * jnp.mean(grad_normed * normed, axis=-1, keepdims=True)
    )
    return (grad_in, jnp.sum(grad_out * normed, axis=0), jnp.sum(grad_out, axis=0))


def rotary_tables(positions):
    half_dims = ROT // 2
    freqs = jnp.power(10000.0, -2.0 * jnp.arange(half_dims).astype(jnp.float32) / ROT)
    angles = positions.astype(jnp.float32)[:, None] * freqs[None, :]
    return (jnp.cos(angles)[:, None, :], jnp.sin(angles)[:, None, :])


def rotate(field_in, positions):
    half_dims = ROT // 2
    cosine, sine = rotary_tables(positions)
    lower = field_in[..., :half_dims]
    upper = field_in[..., half_dims:ROT]
    return jnp.concatenate(
        [lower * cosine - upper * sine, upper * cosine + lower * sine, field_in[..., ROT:]], axis=-1
    )


def rotate_back(field_in, positions):
    half_dims = ROT // 2
    cosine, sine = rotary_tables(positions)
    lower = field_in[..., :half_dims]
    upper = field_in[..., half_dims:ROT]
    return jnp.concatenate(
        [lower * cosine + upper * sine, upper * cosine - lower * sine, field_in[..., ROT:]], axis=-1
    )


def adam_update(grad_in, first_old, second_old, master, rate, decay_rate):
    first_new = beta_one * first_old + (1.0 - beta_one) * grad_in
    second_new = beta_two * second_old + (1.0 - beta_two) * grad_in * grad_in
    root_second = jnp.sqrt(second_new / (1.0 - beta_two**STEP)) + adam_eps
    master_new = (
        master * (1.0 - rate * decay_rate)
        - rate * (first_new / (1.0 - beta_one**STEP)) / root_second
    )
    return (first_new, second_new, master_new)


def shards(
    inputs,
    cotangent,
    joint_weight,
    joint_first,
    joint_second,
    dense_weight,
    dense_first,
    dense_second,
    expand_weight,
    expand_first,
    expand_second,
    shrink_weight,
    shrink_first,
    shrink_second,
    vectors,
    vectors_first,
    vectors_second,
):
    seq_count = lax.axis_size("seq")
    blk_count = lax.axis_size("blk")
    token_rows = inputs.shape[0]
    block_rows = token_rows * seq_count
    local_heads = HEADS // seq_count
    local_width = local_heads * HEAD_DIM
    score_scale = HEAD_DIM ** (-0.5)
    joint_full, dense_full, expand_full, shrink_full, vector_full = (
        lax.all_gather(joint_weight.astype(jnp.bfloat16), ("dp", "seq"), axis=0, tiled=True),
        lax.all_gather(dense_weight.astype(jnp.bfloat16), ("dp", "seq"), axis=0, tiled=True),
        lax.all_gather(expand_weight.astype(jnp.bfloat16), ("dp", "seq"), axis=0, tiled=True),
        lax.all_gather(shrink_weight.astype(jnp.bfloat16), ("dp", "seq"), axis=0, tiled=True),
        lax.all_gather(vectors.astype(jnp.bfloat16), ("dp", "seq"), axis=0, tiled=True),
    )
    vector_wide = vector_full.astype(jnp.float32)
    gain_one = vector_wide[:, 0]
    shift_one = vector_wide[:, 1]
    gain_two = vector_wide[:, 2]
    shift_two = vector_wide[:, 3]
    bias_joint = vector_wide[:, 4:7].T.reshape(3 * D)
    bias_dense = vector_wide[:, 7]
    bias_shrink = vector_wide[:, 8]
    bias_expand = vector_wide[:, 9:].reshape(FF)
    source = inputs.astype(jnp.float32)
    normed_one, hat_one, inv_one = layer_norm(source, gain_one, shift_one)
    normed_one = normed_one.astype(jnp.bfloat16)
    triple = (
        jnp.dot(normed_one, joint_full, preferred_element_type=jnp.float32) + bias_joint
    ).astype(jnp.bfloat16)
    heads_q, heads_k, heads_v = (
        lax.all_to_all(triple[:, 0:D], "seq", split_axis=1, concat_axis=0, tiled=True),
        lax.all_to_all(triple[:, D : 2 * D], "seq", split_axis=1, concat_axis=0, tiled=True),
        lax.all_to_all(triple[:, 2 * D : 3 * D], "seq", split_axis=1, concat_axis=0, tiled=True),
    )
    positions = lax.axis_index("blk") * block_rows + jnp.arange(block_rows)
    queries = rotate(
        heads_q.astype(jnp.float32).reshape(block_rows, local_heads, HEAD_DIM), positions
    ).astype(jnp.bfloat16)
    keys_rot = (
        rotate(heads_k.astype(jnp.float32).reshape(block_rows, local_heads, HEAD_DIM), positions)
        .astype(jnp.bfloat16)
        .reshape(block_rows, local_width)
    )
    last_query = positions[block_rows - 1]
    initial = (
        jnp.full((local_heads, block_rows), masked_score, jnp.float32),
        jnp.zeros((local_heads, block_rows), jnp.float32),
        jnp.zeros((local_heads, block_rows, HEAD_DIM), jnp.float32),
    )
    key_piece = lax.all_gather(keys_rot, "blk", axis=0, tiled=True)
    value_piece = lax.all_gather(heads_v, "blk", axis=0, tiled=True)
    piece_rows = key_piece.shape[0]
    sub_rows = math.gcd(piece_rows, block_rows)
    key_blocks = key_piece.reshape(piece_rows // sub_rows, sub_rows, local_heads, HEAD_DIM)
    value_blocks = value_piece.reshape(piece_rows // sub_rows, sub_rows, local_heads, HEAD_DIM)
    block_starts = sub_rows * jnp.arange(piece_rows // sub_rows)

    def one_block(state_now, block):
        key_block, value_block, first_row = block

        def one_compute(state_old):
            run_max, run_sum, run_acc = state_old
            scores = (
                jnp.einsum("qhd,khd->hqk", queries, key_block, preferred_element_type=jnp.float32)
                * score_scale
            )
            allowed = (first_row + jnp.arange(sub_rows))[None, None, :] <= positions[None, :, None]
            new_max = jnp.maximum(
                run_max, jnp.max(jnp.where(allowed, scores, masked_score), axis=-1)
            )
            exp_terms = jnp.where(allowed, jnp.exp(scores - new_max[..., None]), 0.0)
            factor = jnp.exp(run_max - new_max)
            new_sum = run_sum * factor + jnp.sum(exp_terms, axis=-1)
            new_acc = run_acc * factor[..., None] + jnp.einsum(
                "hqk,khd->hqd",
                exp_terms.astype(jnp.bfloat16),
                value_block,
                preferred_element_type=jnp.float32,
            )
            return (new_max, new_sum, new_acc)

        def one_unchanged(state_old):
            return state_old

        return (lax.cond(first_row > last_query, one_unchanged, one_compute, state_now), None)

    result, unused = lax.scan(one_block, initial, (key_blocks, value_blocks, block_starts))
    run_max, run_sum, run_acc = result
    attended = run_acc / run_sum[..., None]
    log_total = run_max + jnp.log(run_sum)
    attended_rows = (
        jnp.transpose(attended, (1, 0, 2)).reshape(block_rows, local_width).astype(jnp.bfloat16)
    )
    sent_back = lax.all_to_all(attended_rows, "seq", split_axis=0, concat_axis=1, tiled=True)
    attn_out = jnp.dot(sent_back, dense_full, preferred_element_type=jnp.float32) + bias_dense
    normed_two, hat_two, inv_two = layer_norm(source, gain_two, shift_two)
    normed_two = normed_two.astype(jnp.bfloat16)
    expand_pre = jnp.dot(normed_two, expand_full, preferred_element_type=jnp.float32) + bias_expand
    activated = jax.nn.gelu(expand_pre, approximate=False).astype(jnp.bfloat16)
    mlp_out = jnp.dot(activated, shrink_full, preferred_element_type=jnp.float32) + bias_shrink
    output = (source + attn_out + mlp_out).astype(jnp.bfloat16)
    joint_back, dense_back, expand_back, shrink_back = (
        lax.all_gather(joint_weight.astype(jnp.bfloat16), ("dp", "seq"), axis=0, tiled=True),
        lax.all_gather(dense_weight.astype(jnp.bfloat16), ("dp", "seq"), axis=0, tiled=True),
        lax.all_gather(expand_weight.astype(jnp.bfloat16), ("dp", "seq"), axis=0, tiled=True),
        lax.all_gather(shrink_weight.astype(jnp.bfloat16), ("dp", "seq"), axis=0, tiled=True),
    )
    grad_wide = cotangent.astype(jnp.float32)
    grad_act = jnp.dot(cotangent, shrink_back.T, preferred_element_type=jnp.float32)
    unused_gelu, gelu_pull = jax.vjp(partial(jax.nn.gelu, approximate=False), expand_pre)
    grad_pre = gelu_pull(grad_act)[0].astype(jnp.bfloat16)
    grad_shrink = jnp.dot(activated.T, cotangent, preferred_element_type=jnp.float32)
    grad_expand = jnp.dot(normed_two.T, grad_pre, preferred_element_type=jnp.float32)
    grad_normed_two = jnp.dot(grad_pre, expand_back.T, preferred_element_type=jnp.float32)
    grad_dense = jnp.dot(sent_back.T, cotangent, preferred_element_type=jnp.float32)
    grad_bias_out = jnp.sum(grad_wide, axis=0)
    grad_bias_expand = jnp.sum(grad_pre.astype(jnp.float32), axis=0)
    grad_attended = jnp.dot(cotangent, dense_back.T, preferred_element_type=jnp.float32).astype(
        jnp.bfloat16
    )
    heads_grad = lax.all_to_all(grad_attended, "seq", split_axis=1, concat_axis=0, tiled=True)
    grad_heads = heads_grad.reshape(block_rows, local_heads, HEAD_DIM)
    row_delta = jnp.einsum("hqd,qhd->hq", attended, grad_heads.astype(jnp.float32))
    all_keys, all_values = (
        lax.all_gather(keys_rot, "blk", axis=0, tiled=True),
        lax.all_gather(heads_v, "blk", axis=0, tiled=True),
    )
    key_stack = all_keys.reshape(blk_count, block_rows, local_heads, HEAD_DIM)
    value_stack = all_values.reshape(blk_count, block_rows, local_heads, HEAD_DIM)
    own_block = lax.axis_index("blk")

    def key_step(grad_query, block):
        key_block, value_block, block_index = block

        def key_compute(grad_old):
            scores = (
                jnp.einsum("qhd,khd->hqk", queries, key_block, preferred_element_type=jnp.float32)
                * score_scale
            )
            allowed = (block_index * block_rows + jnp.arange(block_rows))[
                None, None, :
            ] <= positions[None, :, None]
            attn_probs = jnp.where(allowed, jnp.exp(scores - log_total[..., None]), 0.0)
            grad_value = jnp.einsum(
                "hqk,qhd->khd",
                attn_probs.astype(jnp.bfloat16),
                grad_heads,
                preferred_element_type=jnp.float32,
            )
            grad_probs = jnp.einsum(
                "qhd,khd->hqk", grad_heads, value_block, preferred_element_type=jnp.float32
            )
            grad_scores = (attn_probs * (grad_probs - row_delta[..., None])).astype(jnp.bfloat16)
            grad_new = grad_old + score_scale * jnp.einsum(
                "hqk,khd->qhd", grad_scores, key_block, preferred_element_type=jnp.float32
            )
            grad_key = score_scale * jnp.einsum(
                "hqk,qhd->khd", grad_scores, queries, preferred_element_type=jnp.float32
            )
            return (grad_new, (grad_key, grad_value))

        def key_unchanged(grad_old):
            empty = jnp.zeros((block_rows, local_heads, HEAD_DIM), jnp.float32)
            return (grad_old, (empty, empty))

        return lax.cond(block_index > own_block, key_unchanged, key_compute, grad_query)

    grad_query, (key_terms, value_terms) = lax.scan(
        key_step,
        jnp.zeros((block_rows, local_heads, HEAD_DIM), jnp.float32),
        (key_stack, value_stack, jnp.arange(blk_count)),
    )
    grad_keys, grad_values = (
        lax.psum_scatter(
            key_terms.reshape(blk_count * block_rows, local_width).astype(jnp.bfloat16),
            "blk",
            scatter_dimension=0,
            tiled=True,
        ).astype(jnp.float32),
        lax.psum_scatter(
            value_terms.reshape(blk_count * block_rows, local_width).astype(jnp.bfloat16),
            "blk",
            scatter_dimension=0,
            tiled=True,
        ).astype(jnp.float32),
    )
    grad_q_pre = (
        rotate_back(grad_query, positions).reshape(block_rows, local_width).astype(jnp.bfloat16)
    )
    grad_k_pre = (
        rotate_back(grad_keys.reshape(block_rows, local_heads, HEAD_DIM), positions)
        .reshape(block_rows, local_width)
        .astype(jnp.bfloat16)
    )
    grad_v_pre = grad_values.astype(jnp.bfloat16)
    token_gq, token_gk, token_gv = (
        lax.all_to_all(grad_q_pre, "seq", split_axis=0, concat_axis=1, tiled=True),
        lax.all_to_all(grad_k_pre, "seq", split_axis=0, concat_axis=1, tiled=True),
        lax.all_to_all(grad_v_pre, "seq", split_axis=0, concat_axis=1, tiled=True),
    )
    grad_triple = jnp.concatenate([token_gq, token_gk, token_gv], axis=1)
    grad_joint = jnp.dot(normed_one.T, grad_triple, preferred_element_type=jnp.float32)
    grad_bias_joint = jnp.sum(grad_triple.astype(jnp.float32), axis=0)
    grad_normed_one = jnp.dot(grad_triple, joint_back.T, preferred_element_type=jnp.float32)
    input_one, grad_gain_one, grad_shift_one = norm_back(
        grad_normed_one, gain_one, hat_one, inv_one
    )
    input_two, grad_gain_two, grad_shift_two = norm_back(
        grad_normed_two, gain_two, hat_two, inv_two
    )
    input_grad = grad_wide + input_one + input_two
    grad_vectors = jnp.concatenate(
        [
            jnp.stack([grad_gain_one, grad_shift_one, grad_gain_two, grad_shift_two], axis=1),
            grad_bias_joint.reshape(3, D).T,
            jnp.stack([grad_bias_out, grad_bias_out], axis=1),
            grad_bias_expand.reshape(D, FF // D),
        ],
        axis=1,
    )
    owned_joint, owned_dense, owned_expand, owned_shrink, owned_vectors = (
        lax.psum_scatter(
            grad_joint.astype(jnp.bfloat16), ("dp", "seq"), scatter_dimension=0, tiled=True
        ).astype(jnp.float32),
        lax.psum_scatter(
            grad_dense.astype(jnp.bfloat16), ("dp", "seq"), scatter_dimension=0, tiled=True
        ).astype(jnp.float32),
        lax.psum_scatter(
            grad_expand.astype(jnp.bfloat16), ("dp", "seq"), scatter_dimension=0, tiled=True
        ).astype(jnp.float32),
        lax.psum_scatter(
            grad_shrink.astype(jnp.bfloat16), ("dp", "seq"), scatter_dimension=0, tiled=True
        ).astype(jnp.float32),
        lax.psum_scatter(
            grad_vectors.astype(jnp.bfloat16), ("dp", "seq"), scatter_dimension=0, tiled=True
        ).astype(jnp.float32),
    )
    total_joint, total_dense, total_expand, total_shrink, total_vectors = (
        lax.psum(owned_joint.astype(jnp.bfloat16), "blk").astype(jnp.float32),
        lax.psum(owned_dense.astype(jnp.bfloat16), "blk").astype(jnp.float32),
        lax.psum(owned_expand.astype(jnp.bfloat16), "blk").astype(jnp.float32),
        lax.psum(owned_shrink.astype(jnp.bfloat16), "blk").astype(jnp.float32),
        lax.psum(owned_vectors.astype(jnp.bfloat16), "blk").astype(jnp.float32),
    )
    joint_m, joint_v, joint_w = adam_update(
        total_joint, joint_first, joint_second, joint_weight, 0.1, weight_decay
    )
    dense_m, dense_v, dense_w = adam_update(
        total_dense, dense_first, dense_second, dense_weight, 1.0, weight_decay
    )
    expand_m, expand_v, expand_w = adam_update(
        total_expand, expand_first, expand_second, expand_weight, 0.1, weight_decay
    )
    shrink_m, shrink_v, shrink_w = adam_update(
        total_shrink, shrink_first, shrink_second, shrink_weight, 0.05, weight_decay
    )
    vector_m, vector_v, vector_w = adam_update(
        total_vectors, vectors_first, vectors_second, vectors, 1.0, 0.0
    )
    return (
        output,
        input_grad,
        joint_m,
        joint_v,
        joint_w,
        dense_m,
        dense_v,
        dense_w,
        expand_m,
        expand_v,
        expand_w,
        shrink_m,
        shrink_v,
        shrink_w,
        vector_m,
        vector_v,
        vector_w,
    )


def solution(mesh):
    return jax.shard_map(
        shards,
        mesh=mesh,
        in_specs=(
            P(("dp", "blk", "seq"), None),
            P(("dp", "blk", "seq"), None),
            P(("dp", "seq"), None),
            P(("dp", "seq"), None),
            P(("dp", "seq"), None),
            P(("dp", "seq"), None),
            P(("dp", "seq"), None),
            P(("dp", "seq"), None),
            P(("dp", "seq"), None),
            P(("dp", "seq"), None),
            P(("dp", "seq"), None),
            P(("dp", "seq"), None),
            P(("dp", "seq"), None),
            P(("dp", "seq"), None),
            P(("dp", "seq"), None),
            P(("dp", "seq"), None),
            P(("dp", "seq"), None),
        ),
        out_specs=(
            P(("dp", "blk", "seq"), None),
            P(("dp", "blk", "seq"), None),
            P(("dp", "seq"), None),
            P(("dp", "seq"), None),
            P(("dp", "seq"), None),
            P(("dp", "seq"), None),
            P(("dp", "seq"), None),
            P(("dp", "seq"), None),
            P(("dp", "seq"), None),
            P(("dp", "seq"), None),
            P(("dp", "seq"), None),
            P(("dp", "seq"), None),
            P(("dp", "seq"), None),
            P(("dp", "seq"), None),
            P(("dp", "seq"), None),
            P(("dp", "seq"), None),
            P(("dp", "seq"), None),
        ),
        check_vma=False,
    )
```

profile of v0, /device:TPU:0, one launch (start us, length us, event | category | flops | bytes accessed | tf_op | source)
XLA Modules:
  0.0 1152.8 jit_solution(11569571177683285889)
XLA Ops:
  11.0 25.3 %all-gather = bf16[16,64,13]{1,2,0:T(8,128)(2,1)S(1)} all-gather(bf16[1,64,13]{1,2,0:T(8,128)(2,1)S(1)} %convert_bitcast_fusion), channel_id=1, replica_groups=mesh['dp'=2,'blk'=8,'seq'=8] {'dp','seq'}, dimensions={0}, use_global_device_ids=true | all-gather | bytes 28288 | tf_op jit(solution)/shard_map/all_gather | solution.py:112
  37.4 40.4 %all-gather.8.cloned.1.call-done = bf16[1024,3072]{1,0:T(8,128)(2,1)} async-done(((bf16[64,3072]{1,0:T(8,128)(2,1)}), bf16[1024,3072]{1,0:T(8,128)(2,1)}) %all-gather.8.cloned.1.call-update) | async-done | bytes 6291472 | tf_op jit(solution)/shard_map/all_gather | solution.py:108
  87.3 6.6 all-to-all-done
  98.1 7.0 all-to-all-done.1
  106.3 11.1 all_to_all.128
  119.3 8.7 all-gather.14.cloned.1.call-done
  136.8 5.7 all-to-all-done.4
  143.6 36.7 %all-gather.10.cloned.1.call-done = bf16[8192,128]{0,1:T(8,128)(2,1)} async-done(((bf16[1024,128]{0,1:T(8,128)(2,1)}), bf16[8192,128]{0,1:T(8,128)(2,1)}) %all-gather.10.cloned.1.call-update) | async-done | bytes 2097168 | tf_op jit(solution)/shard_map/all_gather | solution.py:149
  184.4 48.8 %all-gather.12.cloned.1.call-done = bf16[8192,128]{1,0:T(8,128)(2,1)} async-done(((bf16[1024,128]{1,0:T(8,128)(2,1)}), bf16[8192,128]{1,0:T(8,128)(2,1)}) %all-gather.12.cloned.1.call-update) | async-done | bytes 2097168 | tf_op jit(solution)/shard_map/all_gather | solution.py:150
  233.2 8.2 reshape.295
  241.4 10.7 copy.195
  252.1 24.2 %while.33 = (s32[]{:T(128)}, f32[2,1024]{1,0:T(2,128)S(1)}, f32[2,1024]{1,0:T(2,128)S(1)}, f32[2,1024,64]{1,2,0:T(8,128)S(1)}, s32[8]{0:T(128)S(1)}, /*index=5*/...) while((s32[]{:T(128)}, f32[2,1024]{1,0:T(2,128)S(1)}, ...), condition=%wide.region_7.8_spmd.clone, body=%wide.region_2.7_spmd.clone.sunk | while | flops 561256448 | bytes 31351572 | solution.py:186
  254.0 8.6 conditional.6
  278.2 34.0 %while.34 = (s32[]{:T(128)}, f32[1024,2,64]{0,2,1:T(8,128)S(1)}, bf16[8,1024,2,64]{1,3,2,0:T(8,128)(2,1)}, bf16[8,1024,2,64]{1,3,2,0:T(8,128)(2,1)}, s32[8]{0:T(...) while((s32[]{:T(128)}, f32[1024,2,64]{0,2,1:T(8,128)S(1)}, ...), condition=%wide.region_11.12_spmd.clone, body=%wide.region_8.11_spmd.clone.sunk | while | flops 1364723712 | bytes 72664464 | solution.py:267
  279.6 16.5 %conditional.7 = (f32[1024,2,64]{0,2,1:T(8,128)S(1)}, bf16[1,1024,2,64]{1,3,2,0:T(8,128)(2,1)S(1)}, bf16[1,1024,2,64]{1,3,2,0:T(8,128)(2,1)S(1)}) conditional(s32[]{:T(128)} %convert_element_type.378, (s32[]{:T(128)}, s32[]{:T(128)}, bf16[8,1024,2,64]{1,3,2,0:T(8,128)(2,1)S(1)}, s32[]{:T(128)}, bf16[1024,2,64]{0,2,1:T(8,128)(2,1)S(1)}, ...), branch_computations={%region_9.9_spmd, %region_10.10_spmd} | conditional | flops 1364723712 | bytes 71611032 | solution.py:265
  285.6 5.8 fusion.24
  341.1 41.2 %all-gather.18.cloned.1.call-done = bf16[4096,1024]{1,0:T(8,128)(2,1)} async-done(((bf16[256,1024]{1,0:T(8,128)(2,1)}), bf16[4096,1024]{1,0:T(8,128)(2,1)}) %all-gather.18.cloned.1.call-update) | async-done | bytes 8388624 | tf_op jit(solution)/shard_map/all_gather | solution.py:111
  382.4 10.2 fusion.103
  401.3 5.7 convolution_convert_fusion.1
  407.1 136.0 %reduce-scatter.10.cloned.1.call-done = bf16[1024,128]{0,1:T(8,128)(2,1)} async-done(((bf16[8192,128]{0,1:T(8,128)(2,1)}), bf16[1024,128]{0,1:T(8,128)(2,1)}) %reduce-scatter.10.cloned.1.call-update) | async-done | bytes 262160 | tf_op jit(solution)/shard_map/reduce_scatter | solution.py:273
  549.5 48.4 %reduce-scatter.12.cloned.1.call-done = bf16[1024,128]{0,1:T(8,128)(2,1)} async-done(((bf16[8192,128]{0,1:T(8,128)(2,1)}), bf16[1024,128]{0,1:T(8,128)(2,1)}) %reduce-scatter.12.cloned.1.call-update) | async-done | bytes 262160 | tf_op jit(solution)/shard_map/reduce_scatter | solution.py:279
  605.9 5.8 all-to-all-done.7
  616.3 6.3 all-to-all-done.6
  629.7 7.1 fusion.114
  637.1 6.0 fusion.86
  649.0 24.7 %reduce-scatter.16.cloned.1.call-done = bf16[64,1024]{1,0:T(8,128)(2,1)} async-done(((bf16[1024,1024]{1,0:T(8,128)(2,1)}), bf16[64,1024]{1,0:T(8,128)(2,1)}) %reduce-scatter.16.cloned.1.call-update) | async-done | bytes 131088 | tf_op jit(solution)/shard_map/reduce_scatter | solution.py:324
  673.8 105.9 %reduce-scatter.20.cloned.1.call-done = bf16[256,1024]{1,0:T(8,128)(2,1)} async-done(((bf16[4096,1024]{1,0:T(8,128)(2,1)}), bf16[256,1024]{1,0:T(8,128)(2,1)}) %reduce-scatter.20.cloned.1.call-update) | async-done | bytes 524304 | tf_op jit(solution)/shard_map/reduce_scatter | solution.py:330
  779.7 105.6 %reduce-scatter.18.cloned.1.call-done = bf16[64,4096]{1,0:T(8,128)(2,1)} async-done(((bf16[1024,4096]{1,0:T(8,128)(2,1)}), bf16[64,4096]{1,0:T(8,128)(2,1)}) %reduce-scatter.18.cloned.1.call-update) | async-done | bytes 524304 | tf_op jit(solution)/shard_map/reduce_scatter | solution.py:327
  885.3 92.3 %reduce-scatter.14.cloned.1.call-done = bf16[64,3072]{1,0:T(8,128)(2,1)} async-done(((bf16[1024,3072]{1,0:T(8,128)(2,1)}), bf16[64,3072]{1,0:T(8,128)(2,1)}) %reduce-scatter.14.cloned.1.call-update) | async-done | bytes 393232 | tf_op jit(solution)/shard_map/reduce_scatter | solution.py:321
  981.8 63.7 %reduce-scatter.22.cloned.1.call-done = bf16[64,13]{1,0:T(8,128)(2,1)} async-done(((bf16[1024,13]{1,0:T(8,128)(2,1)}), bf16[64,13]{1,0:T(8,128)(2,1)}) %reduce-scatter.22.cloned.1.call-update) | async-done | bytes 1680
  1046.2 19.1 %psum.39 = bf16[64,13]{0,1:T(8,128)(2,1)S(1)} all-reduce(bf16[64,13]{0,1:T(8,128)(2,1)S(1)} %copy.219), channel_id=1, replica_groups=mesh['dp'=2,'blk'=8,'seq'=8] {'blk'}, use_global_device_ids=true, to_apply=%region_34.35 | all-reduce | flops 832 | bytes 3328 | tf_op jit(solution)/shard_map/psum | solution.py:342
  1066.0 70.7 %all-reduce.3.cloned.1.call-done = (bf16[64,3072]{1,0:T(8,128)(2,1)}, bf16[64,1024]{1,0:T(8,128)(2,1)}, bf16[64,4096]{1,0:T(8,128)(2,1)}, bf16[256,1024]{1,0:T(8,128)(2,1)}) async-done(((bf16[64,3072]{1,0:T(8,128)(2,1)}, bf16[64,1024]{1,0:T(8,128)(2,1)}, bf16[64,4096]{1,0:T(8,128)(2,1)}, bf16[256,1024]{1,0:T(8,128)(2,1)}), (bf16[64,3072]{1,0:T(8,128)(2,1)}, bf16[64,1024]{1,0:T(8,128)(2,1)}, ...) | async-done | bytes 1572880 | tf_op jit(solution)/shard_map/psum | solution.py:338
  (332 shorter events, 157.5 us)
Async XLA Ops:
  7.2 70.6 %all-gather.8.cloned.1.call-start = ((), (), s32[]{:S(2)}) async-start(), calls=%async_computation.15 | async-start | bytes 6684672 | tf_op jit(solution)/shard_map/all_gather | solution.py:108
  9.2 118.8 %all-gather.14.cloned.1.call-start = ((), (), s32[]{:S(2)}) async-start(), calls=%async_computation.18 | async-start | bytes 2228224 | tf_op jit(solution)/shard_map/all_gather | solution.py:109
  82.6 11.4 all-to-all-start
  94.0 11.1 all-to-all-start.1
  97.4 82.9 %all-gather.10.cloned.1.call-start = ((), (), s32[]{:S(2)}) async-start(), calls=%async_computation.16 | async-start | bytes 2359296 | tf_op jit(solution)/shard_map/all_gather | solution.py:149
  106.2 127.0 %all-gather.12.cloned.1.call-start = ((), (), s32[]{:S(2)}) async-start(), calls=%async_computation.17 | async-start | bytes 2359296 | tf_op jit(solution)/shard_map/all_gather | solution.py:150
  117.4 211.3 %all-gather.16.cloned.1.call-start = ((), (), s32[]{:S(2)}) async-start(), calls=%async_computation.19 | async-start | bytes 8912896 | tf_op jit(solution)/shard_map/all_gather | solution.py:110
  118.4 264.0 %all-gather.18.cloned.1.call-start = ((), (), s32[]{:S(2)}) async-start(), calls=%async_computation.20 | async-start | bytes 8912896 | tf_op jit(solution)/shard_map/all_gather | solution.py:111
  131.3 11.3 all-to-all-start.4
  135.0 408.2 %reduce-scatter.10.cloned.1.call-start = ((), (), s32[]{:S(2)}) async-start(), calls=%async_computation.21 | async-start | bytes 2359296 | tf_op jit(solution)/shard_map/reduce_scatter | solution.py:273
  317.7 280.2 %reduce-scatter.12.cloned.1.call-start = ((), (), s32[]{:S(2)}) async-start(), calls=%async_computation.22 | async-start | bytes 2359296 | tf_op jit(solution)/shard_map/reduce_scatter | solution.py:279
  325.0 14.1 %all-to-all-start.3 = ((bf16[8,128,128]{1,2,0:T(8,128)(2,1)}), bf16[8,128,128]{1,2,0:T(8,128)(2,1)S(1)}, u32[]{:S(2)}, u32[]{:S(2)}) async-start(bf16[8,128,128]{1,2,0:T(8,128)(2,1)} %copy.196), calls=%async_computation.3 | async-start | bytes 524288 | tf_op jit(solution)/shard_map/all_to_all | solution.py:193
  328.7 345.1 %reduce-scatter.16.cloned.1.call-start = ((), (), s32[]{:S(2)}) async-start(), calls=%async_computation.24 | async-start | bytes 2228224 | tf_op jit(solution)/shard_map/reduce_scatter | solution.py:324
  341.1 438.6 %reduce-scatter.20.cloned.1.call-start = ((), (), s32[]{:S(2)}) async-start(), calls=%async_computation.26 | async-start | bytes 8912896 | tf_op jit(solution)/shard_map/reduce_scatter | solution.py:330
  400.2 485.1 %reduce-scatter.18.cloned.1.call-start = ((), (), s32[]{:S(2)}) async-start(), calls=%async_computation.25 | async-start | bytes 8912896 | tf_op jit(solution)/shard_map/reduce_scatter | solution.py:327
  407.1 137.1 %copy-start.32 = (f32[1024,8]{0,1:T(8,128)S(1)}, f32[1024,8]{0,1:T(8,128)}, u32[]{:S(2)}) copy-start(f32[1024,8]{0,1:T(8,128)} %copy-done.31) | copy-start | bytes 98308
  407.1 137.1 %copy-start.34 = (f32[1024,8]{0,1:T(8,128)S(1)}, f32[1024,8]{0,1:T(8,128)}, u32[]{:S(2)}) copy-start(f32[1024,8]{0,1:T(8,128)} %copy-done.33) | copy-start | bytes 98308
  545.0 54.6 %all-to-all-start.5 = ((bf16[8,128,128]{1,2,0:T(8,128)(2,1)}), bf16[8,128,128]{1,2,0:T(8,128)(2,1)S(1)}, u32[]{:S(2)}, u32[]{:S(2)}) async-start(bf16[8,128,128]{1,2,0:T(8,128)(2,1)} %copy.202), calls=%async_computation.5 | async-start | bytes 524288 | tf_op jit(solution)/shard_map/all_to_all | solution.py:296
  549.5 73.1 %copy-start.27 = (f32[1024,1]{0,1:T(1,128)S(1)}, f32[1024,1]{0,1:T(1,128)}, u32[]{:S(2)}) copy-start(f32[1024,1]{0,1:T(1,128)} %copy-done.26) | copy-start | bytes 12292
  549.5 73.1 %copy-start.30 = (f32[1024,1]{0,1:T(1,128)S(1)}, f32[1024,1]{0,1:T(1,128)}, u32[]{:S(2)}) copy-start(f32[1024,1]{0,1:T(1,128)} %copy-done.29) | copy-start | bytes 12292
  599.7 12.0 %all-to-all-start.7 = ((bf16[8,128,128]{2,1,0:T(8,128)(2,1)}), bf16[8,128,128]{2,1,0:T(8,128)(2,1)S(1)}, u32[]{:S(2)}, u32[]{:S(2)}) async-start(bf16[8,128,128]{2,1,0:T(8,128)(2,1)} %bitcast.36), calls=%async_computation.9 | async-start | bytes 524288 | tf_op jit(solution)/shard_map/all_to_all | solution.py:298
  611.7 10.9 all-to-all-start.6
  615.1 362.4 %reduce-scatter.14.cloned.1.call-start = ((), (), s32[]{:S(2)}) async-start(), calls=%async_computation.23 | async-start | bytes 6684672 | tf_op jit(solution)/shard_map/reduce_scatter | solution.py:321
  627.2 418.3 %reduce-scatter.22.cloned.1.call-start = ((), (), s32[]{:S(2)}) async-start(), calls=%async_computation.27 | async-start | bytes 278528
  644.0 492.7 %all-reduce.3.cloned.1.call-start = ((), (), s32[]{:S(2)}) async-start(), calls=%async_computation.28 | async-start | bytes 3145728 | tf_op jit(solution)/shard_map/psum | solution.py:338
  644.3 333.3 %copy-start.11 = (bf16[8,128,128]{1,2,0:T(8,128)(2,1)S(1)}, bf16[8,128,128]{1,2,0:T(8,128)(2,1)}, u32[]{:S(2)}) copy-start(bf16[8,128,128]{1,2,0:T(8,128)(2,1)} %copy-done.10) | copy-start | bytes 786436
  644.3 333.3 %copy-start.42 = (f32[1024,1]{0,1:T(1,128)S(1)}, f32[1024,1]{0,1:T(1,128)}, u32[]{:S(2)}) copy-start(f32[1024,1]{0,1:T(1,128)} %get-tuple-element.657) | copy-start | bytes 12292
  977.6 87.7 %copy-start.41 = (f32[64,13]{0,1:T(8,128)S(1)}, f32[64,13]{0,1:T(8,128)}, u32[]{:S(2)}) copy-start(f32[64,13]{0,1:T(8,128)} %param.39) | copy-start | bytes 9988
  977.6 87.7 %copy-start.44 = (f32[64,13]{0,1:T(8,128)S(1)}, f32[64,13]{0,1:T(8,128)}, u32[]{:S(2)}) copy-start(f32[64,13]{0,1:T(8,128)} %param.41) | copy-start | bytes 9988
  977.6 87.7 %copy-start.45 = (f32[64,13]{0,1:T(8,128)S(1)}, f32[64,13]{0,1:T(8,128)}, u32[]{:S(2)}) copy-start(f32[64,13]{0,1:T(8,128)} %param.40) | copy-start | bytes 9988
  977.7 159.1 %copy-start.6 = (f32[256,1024]{1,0:T(8,128)S(1)}, f32[256,1024]{1,0:T(8,128)}, u32[]{:S(2)}) copy-start(f32[256,1024]{1,0:T(8,128)} %param.36) | copy-start | bytes 3145732
  980.6 156.1 %copy-start.19 = (f32[256,1024]{1,0:T(8,128)S(1)}, f32[256,1024]{1,0:T(8,128)}, u32[]{:S(2)}) copy-start(f32[256,1024]{1,0:T(8,128)} %param.38) | copy-start | bytes 3145732
  (37 other events, 361.3 us)
Sparse Core Ops, SparseCore 0:
  11.1 66.7 all-gather.7
  80.9 47.1 all-gather.13
  130.3 49.9 all-gather.9
  181.7 51.3 all-gather.11
  236.0 72.9 all-gather.15
  311.9 70.3 all-gather.17
  384.8 158.3 reduce-scatter.9
  545.6 52.2 reduce-scatter.11
  601.8 71.9 reduce-scatter.15
  678.0 101.6 reduce-scatter.19
  784.0 101.2 reduce-scatter.17
  889.3 88.2 reduce-scatter.13
  981.8 63.5 reduce-scatter.21
  1048.3 88.3 all-reduce.2
where the time goes:
time: 1160 us; the launch traced here: 1150 us
  waiting for transfers between devices  860 us (74%)
  matrix products  80.3 us (7%)
  local copies, waits for them, and re-layouts  69.4 us (6%)
  blocking collectives  55.5 us (5%)
  starting transfers between devices  28.5 us (2%)
  other arithmetic  26.7 us (2%)
  loops' own time  17.4 us (1%)
  between operations  15 us (1%)
    reduce_scatter x1, waiting for transfers between devices, shards(): lax.psum_scatter(key_terms.reshape(blk_count * block_rows, local_width).a...  136 us
    reduce_scatter x1, waiting for transfers between devices, shards(): lax.psum_scatter(grad_shrink.astype(jnp.bfloat16), ('dp', 'seq'), scatter...  106 us
    reduce_scatter x1, waiting for transfers between devices, shards(): lax.psum_scatter(grad_expand.astype(jnp.bfloat16), ('dp', 'seq'), scatter...  106 us
    reduce_scatter x1, waiting for transfers between devices, shards(): lax.psum_scatter(grad_joint.astype(jnp.bfloat16), ('dp', 'seq'), scatter_...  92.3 us
    psum x1, waiting for transfers between devices, shards(): lax.psum(owned_joint.astype(jnp.bfloat16), 'blk').astype(jnp.float32)  70.7 us
    unnamed x15, waiting for transfers between devices  63.9 us
    all_gather x1, waiting for transfers between devices, shards(): value_piece = lax.all_gather(heads_v, 'blk', axis=0, tiled=True)  48.8 us
    reduce_scatter x1, waiting for transfers between devices, shards(): lax.psum_scatter(value_terms.reshape(blk_count * block_rows, local_width)...  48.4 us
  transfers between devices with their start and end apart: 21, of which 19 were waited for; matrix products, arithmetic and copies ran while one was open for 14% of the time, Pallas kernels for 0%

commit v1 on v0

v1 whole, which is shorter than its diff:
```python
from functools import partial

import jax
import jax.numpy as jnp
from jax import lax
from jax.experimental import pallas as pl
from jax.experimental.pallas import tpu as pltpu
from jax.sharding import PartitionSpec as P

D = 1024
HEADS = 16
HEAD_DIM = 64
ROT = 16
FF = 4096
STEP = 10
VCOLS = 13
DP = 2
BLK = 8
SEQ = 8
OWN = 16
ROWS = 128
HALF = 512
BLOCK = 1024
LAST = 15

eps_norm = 1e-05
beta_one = 0.9
beta_two = 0.95
adam_eps = 1e-08
weight_decay = 0.01
masked_score = -1e30

bf16 = jnp.bfloat16
f32 = jnp.float32
MESH = pl.DeviceIdType.MESH
ANY = pl.BlockSpec(memory_space=pl.ANY)
VMEM = pl.BlockSpec(memory_space=pltpu.VMEM)
DMA = pltpu.SemaphoreType.DMA


def remote(src, dst, send_sem, recv_sem, device):
    return pltpu.make_async_remote_copy(
        src_ref=src,
        dst_ref=dst,
        send_sem=send_sem,
        recv_sem=recv_sem,
        device_id=device,
        device_id_type=MESH,
    )


def loop(begin, end, body):
    def step(index, unused):
        body(index)
        return unused

    lax.fori_loop(begin, end, step, jnp.int32(0))


def place():
    return lax.axis_index("dp"), lax.axis_index("blk"), lax.axis_index("seq")


def ring(s):
    return (s + 2) % SEQ, (s + 6) % SEQ, (s + 4) % SEQ, s + 1 - 2 * (s % 2)


def gather_kernel(
    x, c, wj, we, ws, wd, vec, X, C, WJ, WE, WS, WD, VEC, xs, xr, ws_s, ws_r, ds, dr, loc
):
    dp, g, s = place()
    me = dp * SEQ + s
    beside = g + 1 - 2 * (g % 2)

    def peer(p):
        return p // SEQ, jnp.where(p // SEQ == dp, g, beside), p % SEQ

    right, left, across, sibling = ring(s)
    barrier = pltpu.get_barrier_semaphore()

    def greet_peer(t):
        p = (me + t) % OWN
        pl.semaphore_signal(barrier, inc=1, device_id=peer(p), device_id_type=MESH)

    loop(1, OWN, greet_peer)
    pl.semaphore_wait(barrier, OWN - 1)

    def pass_on(source, whole, array, slot, number, target):
        return remote(
            source, whole.at[slot], xs.at[number], xr.at[array, slot], (dp, g, target)
        )

    def first_copies():
        return (
            pass_on(x, X, 0, s, 0, right),
            pass_on(c, C, 1, s, 1, left),
            pass_on(c, C, 1, s, 2, right),
            pass_on(x, X, 0, s, 3, left),
            pass_on(x, X, 0, s, 4, sibling),
            pass_on(c, C, 1, s, 5, sibling),
        )

    def relays():
        return (
            pass_on(X.at[left], X, 0, left, 6, right),
            pass_on(C.at[right], C, 1, right, 7, left),
            pass_on(X.at[left], X, 0, left, 8, sibling),
            pass_on(C.at[right], C, 1, right, 9, sibling),
            pass_on(C.at[left], C, 1, left, 10, sibling),
            pass_on(X.at[right], X, 0, right, 11, sibling),
            pass_on(X.at[across], X, 0, across, 12, sibling),
            pass_on(C.at[across], C, 1, across, 13, sibling),
        )

    def arrive(array, slot):
        source, whole = ((x, X), (c, C))[array]
        pass_on(source, whole, array, slot, 0, sibling).wait_recv()

    def weight_copies(t):
        p = (me + t) % OWN
        target = peer(p)
        return (
            remote(wj.at[p % SEQ], WJ.at[me], ws_s.at[0, t], ws_r.at[0, me], target),
            remote(vec, VEC.at[me], ws_s.at[1, t], ws_r.at[1, me], target),
        )

    def pair_copies():
        target = (1 - dp, beside, s)
        return (
            remote(ws, WS.at[dp], ds.at[0], dr.at[0], target),
            remote(wd, WD.at[dp], ds.at[1], dr.at[1], target),
            remote(we, WE.at[dp], ds.at[2], dr.at[2], target),
        )

    def start_weights(t):
        for copy in weight_copies(t):
            copy.start()

    local = (
        pltpu.make_async_copy(wj.at[s], WJ.at[me], loc.at[0]),
        pltpu.make_async_copy(we, WE.at[dp], loc.at[1]),
        pltpu.make_async_copy(vec, VEC.at[me], loc.at[2]),
        pltpu.make_async_copy(ws, WS.at[dp], loc.at[3]),
        pltpu.make_async_copy(wd, WD.at[dp], loc.at[4]),
        pltpu.make_async_copy(x, X.at[s], loc.at[5]),
        pltpu.make_async_copy(c, C.at[s], loc.at[6]),
    )
    for copy in first_copies():
        copy.start()
    for copy in pair_copies():
        copy.start()
    loop(1, OWN, start_weights)
    for copy in local:
        copy.start()
    relayed = relays()
    arrive(0, left)
    relayed[0].start()
    relayed[2].start()
    arrive(1, right)
    relayed[1].start()
    relayed[3].start()
    arrive(1, left)
    relayed[4].start()
    arrive(0, right)
    relayed[5].start()
    arrive(0, across)
    relayed[6].start()
    arrive(1, across)
    relayed[7].start()
    for copy in local:
        copy.wait()
    for shift in range(0, 8, 2):
        for array in range(2):
            arrive(array, (sibling + shift) % SEQ)

    def take_weight(t):
        p = (me + t) % OWN
        target = peer(p)
        remote(wj.at[0], WJ.at[p], ws_s.at[0, t], ws_r.at[0, p], target).wait_recv()
        remote(vec, VEC.at[p], ws_s.at[1, t], ws_r.at[1, p], target).wait_recv()
        for copy in weight_copies(t):
            copy.wait_send()

    loop(1, OWN, take_weight)
    target = (1 - dp, beside, s)
    remote(ws, WS.at[1 - dp], ds.at[0], dr.at[0], target).wait_recv()
    remote(wd, WD.at[1 - dp], ds.at[1], dr.at[1], target).wait_recv()
    remote(we, WE.at[1 - dp], ds.at[2], dr.at[2], target).wait_recv()
    for copy in first_copies() + relayed + pair_copies():
        copy.wait_send()


def gather(x, c, wj, we, ws, wd, vec):
    def shape(*dims):
        return jax.ShapeDtypeStruct(dims, bf16)

    return pl.pallas_call(
        gather_kernel,
        out_shape=(
            shape(8, ROWS, D),
            shape(8, ROWS, D),
            shape(OWN, 64, 384),
            shape(2, SEQ, 64, 512),
            shape(2, 256, D),
            shape(2, 64, D),
            shape(OWN, 16, 128),
        ),
        in_specs=[ANY] * 7,
        out_specs=(ANY,) * 7,
        scratch_shapes=[
            DMA((14,)),
            DMA((2, 8)),
            DMA((2, OWN)),
            DMA((2, OWN)),
            DMA((3,)),
            DMA((3,)),
            DMA((7,)),
        ],
        compiler_params=pltpu.CompilerParams(collective_id=0, has_side_effects=True),
        name="gather_tokens_weights",
    )(x, c, wj, we, ws, wd, vec)


NT = (((1,), (1,)), ((), ()))
NN = (((1,), (0,)), ((), ()))


def dot(left, right, dims):
    return lax.dot_general(left, right, dims, preferred_element_type=f32)


def low_half(g):
    return jnp.where(g < BLK // 2, 2 * g, LAST - 2 * g)


def attention_kernel(
    q, do, kv, mask, we,
    att, dq, dkv, WE,
    kvall, qs, dos, q2, do2, top, total, acc, lse, delta, dq_acc, stage, sbuf, rbuf, relay,
    att_out, att_in, dq_out, dq_in,
    ks, kr, bs, br, fs, ls, lr, wsend, wrecv, psend, precv, loc,
):
    dp, g, s = place()
    low = low_half(g)
    keep = jnp.where(g < BLK // 2, 0, 1)
    given = 1 - keep
    partner = (dp, BLK - 1 - g, s)
    barrier = pltpu.get_barrier_semaphore()

    def greet(t):
        pl.semaphore_signal(
            barrier, inc=1, device_id=(dp, (g + t) % BLK, s), device_id_type=MESH
        )

    def greet_row(t):
        pl.semaphore_signal(
            barrier, inc=1, device_id=(dp, g, (s + t) % SEQ), device_id_type=MESH
        )

    loop(1, BLK, greet)
    loop(1, SEQ, greet_row)
    pl.semaphore_wait(barrier, BLK + SEQ - 2)

    def swap(number, source, target):
        return remote(source, target, psend.at[number], precv.at[number], partner)

    swap(0, q.at[1], qs.at[keep]).start()
    y, zl = g // 2, g % 2

    def at(dy, z):
        return (y + dy) % 4 * 2 + z

    def order(t):
        k = t // 2
        return jnp.where(k == 2, 3, jnp.where(k == 3, 2, k)), t % 2

    def need(p, j):
        return j <= LAST - low_half(p)

    def send_kv(p, half):
        j = 2 * g + half
        return remote(kv.at[half], kvall.at[j], ks.at[p, half], kr.at[j], (dp, p, s))

    def each_kv(act):
        def step(u):
            dy, dz = order(u // 2 + 1)
            half = u % 2
            z = (zl + dz) % 2
            p, beyond = at(dy, z), at(2, z)
            j = 2 * g + half
            passes = jnp.logical_or(
                jnp.logical_and(dy == 1, half == 0), jnp.logical_and(dy == 3, half == 1)
            )

            @pl.when(jnp.logical_or(need(p, j), jnp.logical_and(passes, need(beyond, j))))
            def _():
                act(send_kv(p, half))

        loop(0, 2 * 5, step)

    def pass_kv(j, half, z, p):
        return remote(
            kvall.at[j], kvall.at[j], fs.at[half, z], kr.at[j], (dp, p, s)
        )

    each_kv(lambda copy: copy.start())
    swap(1, do.at[1], dos.at[keep]).start()
    kvall[2 * g] = kv[0]
    kvall[2 * g + 1] = kv[1]
    qs[keep] = q[0]
    dos[keep] = do[0]

    def weight_copies(t):
        target = (s + t) % SEQ
        return tuple(
            remote(
                we.at[d, target], WE.at[d * SEQ + s], wsend.at[d, t], wrecv.at[d, s], (dp, g, target)
            )
            for d in range(2)
        )

    def start_weights(t):
        for copy in weight_copies(t):
            copy.start()

    local = tuple(
        pltpu.make_async_copy(we.at[d, s], WE.at[d * SEQ + s], loc.at[d]) for d in range(2)
    )
    loop(1, SEQ, start_weights)
    for copy in local:
        copy.start()

    top[...] = jnp.full(top.shape, masked_score, f32)
    total[...] = jnp.zeros(total.shape, f32)
    acc[...] = jnp.zeros(acc.shape, f32)
    dq_acc[...] = jnp.zeros(dq_acc.shape, f32)
    dkv[...] = jnp.zeros(dkv.shape, f32)

    def allowed():
        key_row = lax.broadcasted_iota(jnp.int32, (HALF, HALF), 0)
        query_row = lax.broadcasted_iota(jnp.int32, (HALF, HALF), 1)
        return key_row <= query_row

    swap(0, q.at[1], qs.at[given]).wait_recv()
    for slot in range(2):
        for h in range(2):
            q2[h, slot] = qs[slot] * mask[h]

    def forward_pair(slot, j, diagonal):
        keys = kvall[j, :, 0:128]
        values_t = kvall[j, :, 128:256].T
        for h in range(2):
            scores = dot(keys, q2[h, slot], NT)
            if diagonal:
                scores = jnp.where(allowed(), scores, masked_score)
            old = top[slot, h]
            new = jnp.maximum(old, jnp.max(scores, axis=0, keepdims=True))
            terms = jnp.exp(scores - new)
            factor = jnp.exp(old - new)
            top[slot, h] = new
            total[slot, h] = total[slot, h] * factor + jnp.sum(terms, axis=0, keepdims=True)
            acc[slot, h] = acc[slot, h] * factor + dot(
                values_t[64 * h : 64 * h + 64], terms.astype(bf16), NN
            )

    def both_kinds(pair, slot, j):
        mine = jnp.where(slot == 0, low, LAST - low)

        @pl.when(j < mine)
        def _():
            pair(slot, j, False)

        @pl.when(j == mine)
        def _():
            pair(slot, j, True)

    def passing(dy, half):
        passes = jnp.logical_or(
            jnp.logical_and(dy == 3, half == 0), jnp.logical_and(dy == 1, half == 1)
        )
        return passes, at(jnp.where(half == 0, 1, 3), zl)

    def forward_keys(u):
        dy, dz = order(u // 2)
        half = u % 2
        z = (zl + dz) % 2
        p = at(dy, z)
        j = 2 * p + half
        passes, beyond = passing(dy, half)
        passes = jnp.logical_and(passes, need(beyond, j))

        @pl.when(jnp.logical_and(u >= 2, jnp.logical_or(need(g, j), passes)))
        def _():
            remote(
                kv.at[0], kvall.at[j], ks.at[p, 0], kr.at[j], (dp, p, s)
            ).wait_recv()

        @pl.when(passes)
        def _():
            pass_kv(j, half, z, beyond).start()

        loop(0, 2, lambda slot: both_kinds(forward_pair, slot, j))

    loop(0, 2 * BLK, forward_keys)

    swap(1, do.at[1], dos.at[given]).wait_recv()
    for slot in range(2):
        grads_t = dos[slot].T.astype(f32)
        for h in range(2):
            do2[h, slot] = dos[slot] * mask[h]
            rows = acc[slot, h] / total[slot, h]
            part = slice(64 * h, 64 * h + 64)
            att_out[slot, part] = rows.astype(bf16)
            lse[slot, h] = top[slot, h] + jnp.log(total[slot, h])
            delta[slot, h] = jnp.sum(rows * grads_t[part], axis=0, keepdims=True)
    swap(2, att_out.at[given], att_in).start()
    att[:, 0:HALF] = att_out[keep]

    def backward_pair(slot, j, diagonal):
        keys = kvall[j, :, 0:128]
        values = kvall[j, :, 128:256]
        keys_t = keys.T
        for h in range(2):
            queries = q2[h, slot]
            grads = do2[h, slot]
            scores = dot(keys, queries, NT)
            probs = jnp.exp(scores - lse[slot, h])
            if diagonal:
                probs = jnp.where(allowed(), probs, 0.0)
            grad_probs = dot(values, grads, NT)
            grad_scores = (probs * (grad_probs - delta[slot, h])).astype(bf16)
            stage[:, 128:256] += dot(probs.astype(bf16), grads, NN)
            stage[:, 0:128] += dot(grad_scores, queries, NN)
            dq_acc[slot, h] += dot(keys_t[64 * h : 64 * h + 64], grad_scores, NN)

    def send_back(p, j):
        return remote(
            sbuf.at[j], rbuf.at[g, j % 2], bs.at[j], br.at[g, j % 2], (dp, p, s)
        )

    def step_of(t):
        dy, dz = order(7 - t)
        return dy, (zl + dz) % 2

    def send_far(p, j):
        half = j % 2
        through = at(jnp.where(half == 0, 1, 3), p % 2)
        return remote(
            sbuf.at[j], relay.at[half, zl], bs.at[j], lr.at[half, zl], (dp, through, s)
        )

    def pass_back(half, z):
        source = at(jnp.where(half == 0, 3, 1), z)
        p = at(jnp.where(half == 0, 1, 3), zl)
        copy = remote(
            relay.at[half, z], rbuf.at[source, half], ls.at[half, z], br.at[source, half], (dp, p, s)
        )
        return need(source, 2 * p + half), copy

    def each_pass(act):
        def step(i):
            there, copy = pass_back(i // 2, i % 2)

            @pl.when(there)
            def _():
                act(i // 2, i % 2, copy)

        loop(0, 4, step)

    def start_pass(half, z, copy):
        remote(
            sbuf.at[0], relay.at[half, z], bs.at[0], lr.at[half, z], (dp, at(2 * half + 1, z), s)
        ).wait_recv()
        copy.start()

    def backward_keys(u):
        dy, z = step_of(u // 2)
        p = at(dy, z)
        j = 2 * p + u % 2

        @pl.when(u == 10)
        def _():
            each_pass(start_pass)

        @pl.when(j <= LAST - low)
        def _():
            stage[...] = jnp.zeros(stage.shape, f32)
            loop(0, 2, lambda slot: both_kinds(backward_pair, slot, j))

            @pl.when(p != g)
            def _():
                sbuf[j] = stage[...].astype(bf16)

            @pl.when(jnp.logical_and(p != g, dy != 2))
            def _():
                send_back(p, j).start()

            @pl.when(dy == 2)
            def _():
                send_far(p, j).start()

            @pl.when(p == g)
            def _():
                dkv[u % 2] = stage[...]

    loop(0, 2 * BLK, backward_keys)

    scale = HEAD_DIM ** (-0.5)
    for slot in range(2):
        for h in range(2):
            dq_out[slot, 64 * h : 64 * h + 64] = (dq_acc[slot, h] * scale).astype(bf16)
    swap(3, dq_out.at[given], dq_in).start()
    dq[0] = dq_acc[keep].reshape(128, HALF).T * scale

    def take_back(u):
        p = (g + 1 + u // 2) % BLK
        half = u % 2

        @pl.when(2 * g + half <= LAST - low_half(p))
        def _():
            remote(
                sbuf.at[0], rbuf.at[p, half], bs.at[0], br.at[p, half], (dp, p, s)
            ).wait_recv()
            dkv[half] += rbuf[p, half].astype(f32)

    loop(0, 2 * (BLK - 1), take_back)
    each_kv(lambda copy: copy.wait_send())

    each_pass(lambda half, z, copy: copy.wait_send())

    def sent(u):
        dy, z = step_of(u // 2)
        p = at(dy, z)
        j = 2 * p + u % 2

        @pl.when(need(g, j))
        def _():
            send_back(p, j).wait_send()

    def sent_pass(u):
        dy, dz = order(u // 2)
        half = u % 2
        z = (zl + dz) % 2
        j = 2 * at(dy, z) + half
        passes, beyond = passing(dy, half)

        @pl.when(jnp.logical_and(passes, need(beyond, j)))
        def _():
            pass_kv(j, half, z, beyond).wait_send()

    loop(4, 12, sent_pass)
    loop(0, 2 * (BLK - 1), sent)
    for copy in local:
        copy.wait()

    def take_weights(t):
        source = (s + t) % SEQ
        for d in range(2):
            remote(
                we.at[d, 0], WE.at[d * SEQ + source], wsend.at[d, t], wrecv.at[d, source], (dp, g, source)
            ).wait_recv()
        for copy in weight_copies(t):
            copy.wait_send()

    loop(1, SEQ, take_weights)
    swap(2, att_out.at[given], att_in).wait_recv()
    swap(3, dq_out.at[given], dq_in).wait_recv()
    att[:, HALF:BLOCK] = att_in[...]
    dq[1] = dq_in[...].astype(f32).T
    swap(0, q.at[1], qs.at[keep]).wait_send()
    swap(1, do.at[1], dos.at[keep]).wait_send()
    swap(2, att_out.at[given], att_in).wait_send()
    swap(3, dq_out.at[given], dq_in).wait_send()


def attention(q, do, kv, mask, we):
    return pl.pallas_call(
        attention_kernel,
        out_shape=(
            jax.ShapeDtypeStruct((128, BLOCK), bf16),
            jax.ShapeDtypeStruct((2, HALF, 128), f32),
            jax.ShapeDtypeStruct((2, HALF, 256), f32),
            jax.ShapeDtypeStruct((OWN, 64, 512), bf16),
        ),
        in_specs=[VMEM] * 4 + [ANY],
        out_specs=(VMEM, VMEM, VMEM, ANY),
        scratch_shapes=[
            pltpu.VMEM((16, HALF, 256), bf16),
            pltpu.VMEM((2, HALF, 128), bf16),
            pltpu.VMEM((2, HALF, 128), bf16),
            pltpu.VMEM((2, 2, HALF, 128), bf16),
            pltpu.VMEM((2, 2, HALF, 128), bf16),
            pltpu.VMEM((2, 2, 1, HALF), f32),
            pltpu.VMEM((2, 2, 1, HALF), f32),
            pltpu.VMEM((2, 2, 64, HALF), f32),
            pltpu.VMEM((2, 2, 1, HALF), f32),
            pltpu.VMEM((2, 2, 1, HALF), f32),
            pltpu.VMEM((2, 2, 64, HALF), f32),
            pltpu.VMEM((HALF, 256), f32),
            pltpu.VMEM((16, HALF, 256), bf16),
            pltpu.VMEM((8, 2, HALF, 256), bf16),
            pltpu.VMEM((2, 2, HALF, 256), bf16),
            pltpu.VMEM((2, 128, HALF), bf16),
            pltpu.VMEM((128, HALF), bf16),
            pltpu.VMEM((2, 128, HALF), bf16),
            pltpu.VMEM((128, HALF), bf16),
            DMA((8, 2)),
            DMA((16,)),
            DMA((16,)),
            DMA((8, 2)),
            DMA((2, 2)),
            DMA((2, 2)),
            DMA((2, 2)),
            DMA((2, SEQ)),
            DMA((2, SEQ)),
            DMA((4,)),
            DMA((4,)),
            DMA((2,)),
        ],
        compiler_params=pltpu.CompilerParams(
            collective_id=1, has_side_effects=True, vmem_limit_bytes=48 * 1024 * 1024
        ),
        name="attention_both_ways",
    )(q, do, kv, mask, we)


def scatter_kernel(
    o, h, gj, gd, gv, ge, gs, O, H, RJ, RD, RV, RE, RS, other, sums, halves, ends, ss, sr, hs, hr, es, er, ps, pr, loc
):
    dp, g, s = place()
    me = dp * BLK + g
    right, left, across, sibling = ring(s)
    core = s % 2
    barrier = pltpu.get_barrier_semaphore()
    for target in (right, left, sibling):
        pl.semaphore_signal(barrier, inc=1, device_id=(dp, g, target), device_id_type=MESH)

    def greet_peer(t):
        p = (me + t) % OWN
        pl.semaphore_signal(
            barrier, inc=1, device_id=(p // BLK, p % BLK, s), device_id_type=MESH
        )

    loop(1, OWN, greet_peer)
    pl.semaphore_wait(barrier, 3 + OWN - 1)

    parts = (o, h)

    def to_sibling(a, j):
        piece = 2 * ((s // 2 + j) % 4) + 1 - core
        return remote(
            parts[a].at[piece], other.at[a, j], ss.at[a, j], sr.at[a, j], (dp, g, sibling)
        )

    def across_copies():
        return (
            remote(sums.at[0, 2], halves.at[0], hs.at[0], hr.at[0], (dp, g, right)),
            remote(sums.at[1, 2], halves.at[1], hs.at[1], hr.at[1], (dp, g, left)),
        )

    def end_copies(j):
        target = right if j == 1 else left
        return tuple(
            remote(sums.at[a, j], ends.at[a, j // 2], es.at[a, j // 2], er.at[a, j // 2], (dp, g, target))
            for a in range(2)
        )

    def grad_copies(t):
        p = (me + t) % OWN
        target = (p // BLK, p % BLK, s)
        shard = p // BLK * SEQ + (p % BLK - s + SEQ) % SEQ
        return (
            remote(gj.at[shard], RJ.at[me], ps.at[0, t], pr.at[0, me], target),
            remote(gd.at[p], RD.at[me], ps.at[1, t], pr.at[1, me], target),
            remote(gv.at[shard], RV.at[me], ps.at[2, t], pr.at[2, me], target),
            remote(ge.at[shard], RE.at[me], ps.at[3, t], pr.at[3, me], target),
            remote(gs.at[p], RS.at[me], ps.at[4, t], pr.at[4, me], target),
        )

    def start_grads(t):
        for copy in grad_copies(t):
            copy.start()

    shard = dp * SEQ + (g - s + SEQ) % SEQ
    local = (
        pltpu.make_async_copy(gj.at[shard], RJ.at[me], loc.at[0]),
        pltpu.make_async_copy(gd.at[me], RD.at[me], loc.at[1]),
        pltpu.make_async_copy(gv.at[shard], RV.at[me], loc.at[2]),
        pltpu.make_async_copy(ge.at[shard], RE.at[me], loc.at[3]),
        pltpu.make_async_copy(gs.at[me], RS.at[me], loc.at[4]),
    )
    for j in (2, 1, 3, 0):
        for a in range(2):
            to_sibling(a, j).start()
    loop(1, OWN, start_grads)
    for copy in local:
        copy.start()

    def pair_sum(a, j):
        to_sibling(a, j).wait_recv()
        piece = 2 * ((s // 2 + j) % 4) + core
        return parts[a][piece].astype(f32) + other[a, j].astype(f32)

    halfway = across_copies()
    for a in range(2):
        sums[a, 2] = pair_sum(a, 2).astype(bf16)
        halfway[a].start()
    sums[1, 1] = pair_sum(1, 1).astype(bf16)
    sums[0, 3] = pair_sum(0, 3).astype(bf16)
    end_copies(1)[1].start()
    end_copies(3)[0].start()
    halfway[0].wait_recv()
    sums[0, 1] = (pair_sum(0, 1) + halves[0].astype(f32)).astype(bf16)
    end_copies(1)[0].start()
    halfway[1].wait_recv()
    sums[1, 3] = (pair_sum(1, 3) + halves[1].astype(f32)).astype(bf16)
    end_copies(3)[1].start()
    for a, result in ((0, O), (1, H)):
        own = pair_sum(a, 0)
        end_copies(1)[a].wait_recv()
        own = own + ends[a, 0].astype(f32)
        end_copies(3)[a].wait_recv()
        result[...] = own + ends[a, 1].astype(f32)

    for copy in local:
        copy.wait()

    def take_grads(t):
        p = (me + t) % OWN
        target = (p // BLK, p % BLK, s)
        remote(gj.at[0], RJ.at[p], ps.at[0, t], pr.at[0, p], target).wait_recv()
        remote(gd.at[0], RD.at[p], ps.at[1, t], pr.at[1, p], target).wait_recv()
        remote(gv.at[0], RV.at[p], ps.at[2, t], pr.at[2, p], target).wait_recv()
        remote(ge.at[0], RE.at[p], ps.at[3, t], pr.at[3, p], target).wait_recv()
        remote(gs.at[0], RS.at[p], ps.at[4, t], pr.at[4, p], target).wait_recv()
        for copy in grad_copies(t):
            copy.wait_send()

    loop(1, OWN, take_grads)
    for j in range(4):
        for a in range(2):
            to_sibling(a, j).wait_send()
    for copy in halfway + end_copies(1) + end_copies(3):
        copy.wait_send()


def scatter(o, h, gj, gd, gv, ge, gs):
    piece = jax.ShapeDtypeStruct((ROWS, D), f32)
    return pl.pallas_call(
        scatter_kernel,
        out_shape=(piece, piece)
        + tuple(jax.ShapeDtypeStruct(a.shape, a.dtype) for a in (gj, gd, gv, ge, gs)),
        in_specs=[VMEM] * 2 + [ANY] * 5,
        out_specs=(VMEM, VMEM) + (ANY,) * 5,
        scratch_shapes=[
            pltpu.VMEM((2, 4, ROWS, D), bf16),
            pltpu.VMEM((2, 4, ROWS, D), bf16),
            pltpu.VMEM((2, ROWS, D), bf16),
            pltpu.VMEM((2, 2, ROWS, D), bf16),
            DMA((2, 4)),
            DMA((2, 4)),
            DMA((2,)),
            DMA((2,)),
            DMA((2, 2)),
            DMA((2, 2)),
            DMA((5, OWN)),
            DMA((5, OWN)),
            DMA((5,)),
        ],
        compiler_params=pltpu.CompilerParams(
            collective_id=2, has_side_effects=True, vmem_limit_bytes=40 * 1024 * 1024
        ),
        name="scatter_sums",
    )(o, h, gj, gd, gv, ge, gs)


def spread_kernel(rj, re, rv, rs, rd, FJ, FE, FV, FS, FD, as_, ar, bs, br, loc):
    dp, g, s = place()
    owner = (g - s + SEQ) % SEQ
    own = jnp.where(owner == s, 1, 0)
    barrier = pltpu.get_barrier_semaphore()

    def source(t):
        k = (s + t) % SEQ
        return (dp, (s + k) % BLK, k), k

    def greet(t):
        @pl.when(jnp.logical_or(t > 0, own == 0))
        def _():
            pl.semaphore_signal(barrier, inc=1, device_id=source(t)[0], device_id_type=MESH)

        @pl.when(t > 0)
        def _():
            pl.semaphore_signal(
                barrier, inc=1, device_id=(dp, (g + t) % BLK, s), device_id_type=MESH
            )

    loop(0, 8, greet)
    pl.semaphore_wait(barrier, 8 - own + 7)

    def row_copies(t):
        target = (dp, (g + t) % BLK, owner)
        return (
            remote(rj, FJ.at[s], as_.at[0, t], ar.at[0, s], target),
            remote(re, FE.at[s], as_.at[1, t], ar.at[1, s], target),
            remote(rv, FV.at[s], as_.at[2, t], ar.at[2, s], target),
        )

    def column_copies(t):
        target = (dp, (g + t) % BLK, s)
        return (
            remote(rs, FS.at[g], bs.at[0, t], br.at[0, g], target),
            remote(rd, FD.at[g], bs.at[1, t], br.at[1, g], target),
        )

    local_rows = (
        pltpu.make_async_copy(rj, FJ.at[s], loc.at[0]),
        pltpu.make_async_copy(re, FE.at[s], loc.at[1]),
        pltpu.make_async_copy(rv, FV.at[s], loc.at[2]),
    )
    local = (
        pltpu.make_async_copy(rs, FS.at[g], loc.at[3]),
        pltpu.make_async_copy(rd, FD.at[g], loc.at[4]),
    )

    def start(t):
        @pl.when(jnp.logical_or(t > 0, own == 0))
        def _():
            for copy in row_copies(t):
                copy.start()

        @pl.when(t > 0)
        def _():
            for copy in column_copies(t):
                copy.start()

    loop(0, 8, start)
    for copy in local:
        copy.start()

    @pl.when(own == 1)
    def _():
        for copy in local_rows:
            copy.start()
        for copy in local_rows:
            copy.wait()

    for copy in local:
        copy.wait()

    def take(t):
        @pl.when(jnp.logical_or(t > 0, own == 0))
        def _():
            target, k = source(t)
            remote(rj, FJ.at[k], as_.at[0, t], ar.at[0, k], target).wait_recv()
            remote(re, FE.at[k], as_.at[1, t], ar.at[1, k], target).wait_recv()
            remote(rv, FV.at[k], as_.at[2, t], ar.at[2, k], target).wait_recv()
            for copy in row_copies(t):
                copy.wait_send()

        @pl.when(t > 0)
        def _():
            k = (g + t) % BLK
            target = (dp, k, s)
            remote(rs, FS.at[k], bs.at[0, t], br.at[0, k], target).wait_recv()
            remote(rd, FD.at[k], bs.at[1, t], br.at[1, k], target).wait_recv()
            for copy in column_copies(t):
                copy.wait_send()

    loop(0, 8, take)


def spread(*parts):
    return pl.pallas_call(
        spread_kernel,
        out_shape=tuple(jax.ShapeDtypeStruct((8,) + a.shape, a.dtype) for a in parts),
        in_specs=[ANY] * 5,
        out_specs=(ANY,) * 5,
        scratch_shapes=[DMA((3, 8)), DMA((3, 8)), DMA((2, 8)), DMA((2, 8)), DMA((5,))],
        compiler_params=pltpu.CompilerParams(collective_id=3, has_side_effects=True),
        name="spread_gradients",
    )(*parts)


def rotary_tables(positions):
    half_dims = ROT // 2
    freqs = jnp.power(10000.0, -2.0 * jnp.arange(half_dims).astype(f32) / ROT)
    angles = positions.astype(f32)[:, None] * jnp.tile(freqs, 128 // half_dims)[None, :]
    dim = (jnp.arange(128) % HEAD_DIM)[None, :]
    own = jnp.where(dim < ROT, jnp.cos(angles), 1.0)
    swapped = jnp.where(dim < half_dims, -jnp.sin(angles), jnp.sin(angles))
    return own, jnp.where(dim < ROT, swapped, 0.0)


def exchange():
    half_dims = ROT // 2
    lane = jnp.arange(128)
    dim = lane % HEAD_DIM
    source = jnp.where(dim < half_dims, lane + half_dims, lane - half_dims)
    return ((lane[:, None] == source[None, :]) & (dim < ROT)[None, :]).astype(f32)


def rotate(rows, own, swapped):
    other = jnp.dot(
        rows, exchange().astype(rows.dtype), precision=lax.Precision.HIGHEST,
        preferred_element_type=f32,
    )
    return rows.astype(f32) * own + other * swapped


def adam_update(grad_in, first_old, second_old, master, rate, decay_rate):
    first_new = beta_one * first_old + (1.0 - beta_one) * grad_in
    second_new = beta_two * second_old + (1.0 - beta_two) * grad_in * grad_in
    root_second = jnp.sqrt(second_new / (1.0 - beta_two**STEP)) + adam_eps
    master_new = (
        master * (1.0 - rate * decay_rate)
        - rate * (first_new / (1.0 - beta_one**STEP)) / root_second
    )
    return (first_new, second_new, master_new)


def norm_stats(source):
    centred = source - jnp.mean(source, axis=-1, keepdims=True)
    inv_std = lax.rsqrt(jnp.mean(centred * centred, axis=-1, keepdims=True) + eps_norm)
    return centred * inv_std, inv_std


def shards(
    inputs,
    cotangent,
    joint_weight,
    joint_first,
    joint_second,
    dense_weight,
    dense_first,
    dense_second,
    expand_weight,
    expand_first,
    expand_second,
    shrink_weight,
    shrink_first,
    shrink_second,
    vectors,
    vectors_first,
    vectors_second,
):
    dp, g, s = place()
    wj = joint_weight.astype(bf16).reshape(64, 3, 2, SEQ, 64)
    wj = jnp.transpose(wj, (3, 0, 1, 2, 4)).reshape(SEQ, 64, 384)
    we = expand_weight.astype(bf16).reshape(64, 2, SEQ, 256)
    we = jnp.transpose(we, (2, 0, 1, 3)).reshape(SEQ, 64, 512)
    vec = jnp.concatenate([vectors[:, :9].T.reshape(576), vectors[:, 9:].reshape(256)])
    vec = jnp.pad(vec.astype(bf16), (0, 2048 - 832)).reshape(16, 128)
    X, C, WJ, WE, WS, WD, VEC = gather(
        inputs, cotangent, wj, we, shrink_weight.astype(bf16), dense_weight.astype(bf16), vec
    )
    X = X.reshape(BLOCK, D)
    C = C.reshape(BLOCK, D)
    WJ = WJ.reshape(D, 384)
    WS = WS.reshape(512, D)
    WD = WD.reshape(128, D)
    VEC = VEC.reshape(OWN, 2048).astype(f32)
    table = jnp.swapaxes(VEC[:, :576].reshape(OWN, 9, 64), 0, 1).reshape(9, D)
    gain_one, shift_one, gain_two, shift_two = (table[i] for i in range(4))
    bias_joint = jnp.take(table[4:7].reshape(3, 2, SEQ, 64), s, axis=2).reshape(384)
    bias_out = table[7] + table[8]
    bias_expand = jnp.take(VEC[:, 576:832].reshape(2, SEQ, 256), s, axis=1).reshape(512)

    hat, _ = norm_stats(X.astype(f32))
    normed_one = (hat * gain_one + shift_one).astype(bf16)
    normed_two = (hat * gain_two + shift_two).astype(bf16)
    triple = (jnp.dot(normed_one, WJ, preferred_element_type=f32) + bias_joint).astype(bf16)
    positions = g * BLOCK + jnp.arange(BLOCK)
    cosine, sine = rotary_tables(positions)
    queries = rotate(triple[:, 0:128], cosine, sine).astype(bf16)
    keys = rotate(triple[:, 128:256], cosine, sine).astype(bf16)
    kv = jnp.concatenate([keys, triple[:, 256:]], axis=1).reshape(2, HALF, 256)
    grad_att = lax.dot_general(C, WD, NT, preferred_element_type=f32).astype(bf16)

    scaled = (queries.astype(f32) * HEAD_DIM ** (-0.5)).astype(bf16)
    lane = jnp.arange(128)
    mask = jnp.stack([lane < 64, lane >= 64]).astype(bf16).reshape(2, 1, 128)
    att, dq, dkv, WE = attention(
        scaled.reshape(2, HALF, 128),
        grad_att.reshape(2, HALF, 128),
        kv,
        mask,
        WE,
    )
    WE = WE.reshape(D, 512)

    expand_pre = jnp.dot(normed_two, WE, preferred_element_type=f32) + bias_expand
    activated, gelu_pull = jax.vjp(partial(jax.nn.gelu, approximate=False), expand_pre)
    activated = activated.astype(bf16)
    mlp_part = jnp.dot(activated, WS, preferred_element_type=f32)
    grad_act = lax.dot_general(C, WS, NT, preferred_element_type=f32)
    grad_pre = gelu_pull(grad_act)[0].astype(bf16)
    grad_shrink = jnp.dot(activated.T, C, preferred_element_type=f32).astype(bf16)
    grad_expand = jnp.dot(normed_two.T, grad_pre, preferred_element_type=f32).astype(bf16)

    grad_normed_two = lax.dot_general(grad_pre, WE, NT, preferred_element_type=f32)
    out_part = lax.dot_general(att, WD, (((0,), (0,)), ((), ())), preferred_element_type=f32)
    out_part = (out_part + mlp_part).astype(bf16)
    grad_dense = jnp.dot(att, C, preferred_element_type=f32).astype(bf16)
    grad_q = rotate(dq.reshape(BLOCK, 128), cosine, -sine)
    dkv = dkv.reshape(BLOCK, 256)
    grad_k = rotate(dkv[:, :128], cosine, -sine)
    grad_triple = jnp.concatenate([grad_q, grad_k, dkv[:, 128:]], axis=1).astype(bf16)
    grad_joint = jnp.dot(normed_one.T, grad_triple, preferred_element_type=f32).astype(bf16)
    grad_normed_one = lax.dot_general(grad_triple, WJ, NT, preferred_element_type=f32)
    grad_hat = (grad_normed_one * gain_one + grad_normed_two * gain_two).astype(bf16)

    first = jnp.where(s == 0, 1.0, 0.0)
    grad_bias_out = first * jnp.sum(C.astype(f32), axis=0)
    mine = (jnp.arange(SEQ) == s).astype(f32)
    grad_bias_joint = jnp.sum(grad_triple.astype(f32), axis=0).reshape(3, 2, 1, 64)
    grad_bias_joint = (grad_bias_joint * mine[None, None, :, None]).reshape(3, D)
    grad_bias_expand = jnp.sum(grad_pre.astype(f32), axis=0).reshape(2, 1, 256)
    grad_bias_expand = (grad_bias_expand * mine[None, :, None]).reshape(OWN, 256)
    grad_rows = jnp.concatenate(
        [
            jnp.sum(grad_normed_one * hat, axis=0)[None],
            jnp.sum(grad_normed_one, axis=0)[None],
            jnp.sum(grad_normed_two * hat, axis=0)[None],
            jnp.sum(grad_normed_two, axis=0)[None],
            grad_bias_joint,
            grad_bias_out[None],
            grad_bias_out[None],
        ]
    )
    grad_rows = jnp.swapaxes(grad_rows.reshape(9, OWN, 64), 0, 1).reshape(OWN, 576)
    gv = jnp.pad(jnp.concatenate([grad_rows, grad_bias_expand], axis=1), ((0, 0), (0, 192)))
    gd = jnp.transpose(grad_dense.reshape(2, 64, BLK, 128), (0, 2, 1, 3)).reshape(OWN, 64, 128)

    O, H, RJ, RD, RV, RE, RS = scatter(
        out_part.reshape(8, ROWS, D),
        grad_hat.reshape(8, ROWS, D),
        grad_joint.reshape(OWN, 64, 384),
        gd,
        gv.reshape(OWN, 8, 128),
        grad_expand.reshape(OWN, 64, 512),
        grad_shrink.reshape(OWN, 32, D),
    )

    def total(parts):
        return jnp.sum(parts.astype(f32), axis=0)

    FJ, FE, FV, FS, FD = spread(
        total(RJ).astype(bf16),
        total(RE).astype(bf16),
        total(RV),
        total(RS).astype(bf16),
        total(RD).astype(bf16),
    )

    source = inputs.astype(f32)
    output = (source + O + bias_out).astype(bf16)
    own_hat, own_inv = norm_stats(source)
    own_grad = H
    input_grad = cotangent.astype(f32) + own_inv * (
        own_grad
        - jnp.mean(own_grad, axis=-1, keepdims=True)
        - own_hat * jnp.mean(own_grad * own_hat, axis=-1, keepdims=True)
    )

    total_joint = jnp.transpose(FJ.reshape(SEQ, 64, 3, 2, 64), (1, 2, 3, 0, 4)).reshape(64, 3 * D)
    total_expand = jnp.transpose(FE.reshape(SEQ, 64, 2, 256), (1, 2, 0, 3)).reshape(64, FF)
    total_shrink = FS.reshape(256, D)
    total_dense = jnp.transpose(FD, (1, 0, 2)).reshape(64, D)
    sums = jnp.sum(FV, axis=0).reshape(1024)
    total_vectors = jnp.concatenate(
        [sums[:576].reshape(9, 64).T, sums[576:832].reshape(64, 4)], axis=1
    )
    joint = adam_update(
        total_joint.astype(f32), joint_first, joint_second, joint_weight, 0.1, weight_decay
    )
    dense = adam_update(
        total_dense.astype(f32), dense_first, dense_second, dense_weight, 1.0, weight_decay
    )
    expand = adam_update(
        total_expand.astype(f32), expand_first, expand_second, expand_weight, 0.1, weight_decay
    )
    shrink = adam_update(
        total_shrink.astype(f32), shrink_first, shrink_second, shrink_weight, 0.05, weight_decay
    )
    vector = adam_update(total_vectors, vectors_first, vectors_second, vectors, 1.0, 0.0)
    return (output, input_grad) + joint + dense + expand + shrink + vector


def solution(mesh):
    return jax.shard_map(
        shards,
        mesh=mesh,
        in_specs=(
            P(("dp", "blk", "seq"), None),
            P(("dp", "blk", "seq"), None),
            P(("dp", "seq"), None),
            P(("dp", "seq"), None),
            P(("dp", "seq"), None),
            P(("dp", "seq"), None),
            P(("dp", "seq"), None),
            P(("dp", "seq"), None),
            P(("dp", "seq"), None),
            P(("dp", "seq"), None),
            P(("dp", "seq"), None),
            P(("dp", "seq"), None),
            P(("dp", "seq"), None),
            P(("dp", "seq"), None),
            P(("dp", "seq"), None),
            P(("dp", "seq"), None),
            P(("dp", "seq"), None),
        ),
        out_specs=(
            P(("dp", "blk", "seq"), None),
            P(("dp", "blk", "seq"), None),
            P(("dp", "seq"), None),
            P(("dp", "seq"), None),
            P(("dp", "seq"), None),
            P(("dp", "seq"), None),
            P(("dp", "seq"), None),
            P(("dp", "seq"), None),
            P(("dp", "seq"), None),
            P(("dp", "seq"), None),
            P(("dp", "seq"), None),
            P(("dp", "seq"), None),
            P(("dp", "seq"), None),
            P(("dp", "seq"), None),
            P(("dp", "seq"), None),
            P(("dp", "seq"), None),
            P(("dp", "seq"), None),
        ),
        check_vma=False,
    )
```

time: 1160 us -> 379 us (0.33)
  waiting for transfers between devices: 860 us -> 0 us
  Pallas kernels: 0 us -> 278 us
  blocking collectives: 55.5 us -> 0 us
  local copies, waits for them, and re-layouts: 69.4 us -> 20.4 us
  matrix products: 80.3 us -> 38 us
  starting transfers between devices: 28.5 us -> 0 us
  loops' own time: 17.4 us -> 0 us
  between operations: 15 us -> 1.78 us
    reduce_scatter x6 -> x0, waiting for transfers between devices: 513 us -> none  [the longest x1 136 us: shards(): lax.psum_scatter(key_terms.reshape(blk_count * block_rows, local_width).a...]
    pallas_call x0 -> x4, Pallas kernels: none -> 278 us  [the longest x1 122 us: attention(): pl.pallas_call(attention_kernel, out_shape=(jax.ShapeDtypeStruct((128, BL...]
    all_gather x6 -> x0, waiting for transfers between devices: 176 us -> none  [the longest x1 48.8 us: shards(): value_piece = lax.all_gather(heads_v, 'blk', axis=0, tiled=True)]
    psum x1 -> x0, waiting for transfers between devices: 70.7 us -> none  [shards(): lax.psum(owned_joint.astype(jnp.bfloat16), 'blk').astype(jnp.float32)]
    unnamed x15 -> x0, waiting for transfers between devices: 63.9 us -> none
    dot_general x19 -> x16, matrix products: 80.3 us -> 38 us  [the longest x4 10 us: rotate(): jnp.dot(rows, exchange().astype(rows.dtype), precision=lax.Precision.HIGH...]
    all_to_all x7 -> x0, waiting for transfers between devices: 36.7 us -> none  [the longest x1 6.96 us: shards(): lax.all_to_all(triple[:, 0:D], 'seq', split_axis=1, concat_axis=0, tiled=...]
    all_to_all x7 -> x0, starting transfers between devices: 26.6 us -> none  [the longest x1 4.46 us: shards(): lax.all_to_all(grad_v_pre, 'seq', split_axis=0, concat_axis=1, tiled=True)]
  transfers between devices with their start and end apart: 21 -> 0, of which waited for: 19 -> 0; matrix products, arithmetic and copies ran while one was open for 14% -> 0% of each run, Pallas kernels for 0% -> 0%
where the time goes in v1:
time: 379 us; the launch traced here: 374 us
  Pallas kernels  278 us (73%)
  matrix products  38 us (10%)
  other arithmetic  35.7 us (9%)
  local copies, waits for them, and re-layouts  20.4 us (5%)
    pallas_call x1, Pallas kernels, attention(): pl.pallas_call(attention_kernel, out_shape=(jax.ShapeDtypeStruct((128, BL...  122 us
    pallas_call x1, Pallas kernels, gather(): pl.pallas_call(gather_kernel, out_shape=(shape(8, ROWS, D), shape(8, ROWS...  63.1 us
    pallas_call x1, Pallas kernels, scatter(): pl.pallas_call(scatter_kernel, out_shape=(piece, piece) + tuple((jax.Shap...  61.8 us
    pallas_call x1, Pallas kernels, spread(): pl.pallas_call(spread_kernel, out_shape=tuple((jax.ShapeDtypeStruct((8,)...  31.3 us
    sub x5, other arithmetic, adam_update(): master * (1.0 - rate * decay_rate)  10.1 us
    dot_general x4, matrix products, rotate(): jnp.dot(rows, exchange().astype(rows.dtype), precision=lax.Precision.HIGH...  10 us
    dot_general x1, matrix products, shards(): grad_act = lax.dot_general(C, WS, NT, preferred_element_type=f32)  7.82 us

profile of v1, /device:TPU:0, one launch (start us, length us, event | category | flops | bytes accessed | tf_op | source)
XLA Modules:
  0.0 373.6 jit_solution(4283395333231755099)
XLA Ops:
  5.4 1.6 convert_element_type.219.wd
  7.0 1.2 convert_element_type.216
  9.3 1.2 reshape.419.wj
  13.2 63.1 %gather_tokens_weights.1 = (bf16[8,128,1024]{2,1,0:T(8,128)(2,1)}, bf16[8,128,1024]{2,1,0:T(8,128)(2,1)}, bf16[16,64,384]{2,1,0:T(8,128)(2,1)}, bf16[2,8,64,512]...) custom-call(bf16[128,1024]{1,0:T(8,128)(2,1)} %x.5, ...), custom_call_target="tpu_custom_call" | custom-call | tf_op jit(solution)/shard_map/gather_tokens_weights/pallas_call | solution.py:197
  76.3 2.1 convert_reduce_fusion.1
  78.5 2.6 convert_reduce_fusion
  83.6 1.3 add_convert_fusion.4
  85.0 1.3 add_convert_fusion.7
  86.3 2.4 fusion.11
  88.7 2.5 fusion.15
  91.3 121.6 %attention_both_ways.1 = (bf16[128,1024]{1,0:T(8,128)(2,1)S(1)}, f32[2,512,128]{2,1,0:T(8,128)S(1)}, f32[2,512,256]{2,1,0:T(8,128)S(1)}, bf16[16,64,512]{2,1,0:T(8,128)(2,1)S(1)}) custom-call(bf16[2,512,128]{2,1,0:T(8,128)(2,1)S(1)} %bitcast.135, bf16[2,512,128]{2,1,0:T(8,128)(2,1)S(1)} %bitcast.132, bf16[2,512,256]{2,1,0:T(8,128)(2,1)S(1)} %bitcast.129, ...), custom_call_target="tpu_custom_call" | custom-call | tf_op jit(solution)/shard_map/attention_both_ways/pallas_call | solution.py:577
  212.9 2.6 fusion.80
  215.5 2.5 fusion.16
  218.0 2.6 fusion.17
  224.2 7.8 %convert_reduce_fusion.2 = (f32[512]{0:T(512)S(1)}, bf16[1024,512]{1,0:T(8,128)(2,1)}, f32[1024,512]{1,0:T(8,128)S(1)}) fusion(f32[1024,512]{1,0:T(8,128)S(1)} %copy-done.25, f32[512]{0:T(512)S(1)} %bitcast.169, bf16[1024,1024]{1,0:T(8,128)(2,1)S(1)} %bitcast.143, bf16[512,1024]{1,0:T(8,128)(2,1)} %bitcast.158), kind=kOutput, calls=%fused_computation.15 | convolution fusion | flops 1113062912 | bytes 8392704 | tf_op jit(solution)/shard_map/dot_general | solution.py:996
  232.7 1.3 convolution_convert_fusion
  234.7 2.8 fusion.67
  237.5 3.6 fusion.68
  241.1 2.2 convolution_convert_fusion.2
  243.3 2.2 convolution_convert_fusion.1
  250.8 1.8 fusion.79
  252.7 1.3 add_convert_fusion.3
  254.2 61.8 %scatter_sums.1 = (f32[128,1024]{1,0:T(8,128)S(1)}, f32[128,1024]{1,0:T(8,128)S(1)}, bf16[16,64,384]{2,1,0:T(8,128)(2,1)S(1)}, bf16[16,64,128]{2,1,0:T(8,128)(2,...) custom-call(bf16[8,128,1024]{2,1,0:T(8,128)(2,1)S(1)} %bitcast.126, ...), custom_call_target="tpu_custom_call" | custom-call | tf_op jit(solution)/shard_map/scatter_sums/pallas_call | solution.py:749
  316.3 1.5 fusion.30
  319.1 1.9 reduce_sum.196.rj
  321.0 2.0 reduce_sum.197.re
  323.8 31.3 %spread_gradients.1 = (bf16[8,64,384]{2,1,0:T(8,128)(2,1)}, bf16[8,64,512]{2,1,0:T(8,128)(2,1)}, f32[8,8,128]{2,1,0:T(8,128)}, bf16[8,32,1024]{2,1,0:T(8,128)(2,1)}, bf16[8,64,128]{2,1,0:T(8,128)(2,1)}) custom-call(bf16[64,384]{1,0:T(8,128)(2,1)} %reduce_sum.196.rj, bf16[64,512]{1,0:T(8,128)(2,1)} %reduce_sum.197.re, f32[8,128]{1,0:T(8,128)} %reduce_sum.198.rv, ...), custom_call_target="tpu_custom_call" | custom-call | tf_op jit(solution)/shard_map/spread_gradients/pallas_call | solution.py:874
  356.9 1.9 divide_subtract_fusion.3
  360.1 1.6 copy.64
  364.7 3.2 divide_subtract_fusion.2
  368.1 2.1 divide_subtract_fusion.1
  371.1 2.2 divide_subtract_fusion
  (192 shorter events, 30.8 us)
Async XLA Ops:
  8.2 2.4 copy-start.17
  78.5 2.7 copy-start.44
  78.5 3.5 copy-start.28
  88.7 2.5 copy-start.5
  212.9 2.6 copy-start.8
  218.0 2.6 copy-start.29
  218.0 5.0 %copy-start.11 = (bf16[8,128,1024]{2,1,0:T(8,128)(2,1)S(1)}, bf16[8,128,1024]{2,1,0:T(8,128)(2,1)}, u32[]{:S(2)}) copy-start(bf16[8,128,1024]{2,1,0:T(8,128)(2,1)} %get-tuple-element.43) | copy-start | bytes 6291460
  234.7 2.8 copy-start.9
  234.7 2.8 copy-start.13
  234.7 2.8 copy-start.51
  237.5 3.6 copy-start.24
  237.5 3.6 copy-start.30
  237.5 3.6 copy-start.32
  254.2 61.8 %copy-start.16 = (bf16[128,1024]{1,0:T(8,128)(2,1)S(1)}, bf16[128,1024]{1,0:T(8,128)(2,1)}, u32[]{:S(2)}) copy-start(bf16[128,1024]{1,0:T(8,128)(2,1)} %x.5) | copy-start | bytes 786436
  254.2 61.8 %copy-start.49 = (f32[128]{0:T(128)S(1)}, f32[128]{0:T(128)}, u32[]{:S(2)}) copy-start(f32[128]{0:T(128)} %copy-done.48) | copy-start | bytes 1540
  254.2 61.8 %copy-start.50 = (f32[128]{0:T(128)S(1)}, f32[128]{0:T(128)}, u32[]{:S(2)}) copy-start(f32[128]{0:T(128)} %add_rsqrt_fusion.1) | copy-start | bytes 1540
  254.2 62.1 %copy-start.37 = (bf16[128,1024]{1,0:T(8,128)(2,1)S(1)}, bf16[128,1024]{1,0:T(8,128)(2,1)}, u32[]{:S(2)}) copy-start(bf16[128,1024]{1,0:T(8,128)(2,1)} %c.1) | copy-start | bytes 786436
  317.7 38.5 %copy-start.45 = (f32[64,13]{0,1:T(8,128)S(1)}, f32[64,13]{0,1:T(8,128)}, u32[]{:S(2)}) copy-start(f32[64,13]{0,1:T(8,128)} %param.31) | copy-start | bytes 9988
  317.7 38.5 %copy-start.46 = (f32[64,13]{0,1:T(8,128)S(1)}, f32[64,13]{0,1:T(8,128)}, u32[]{:S(2)}) copy-start(f32[64,13]{0,1:T(8,128)} %param.33) | copy-start | bytes 9988
  317.8 38.5 %copy-start.47 = (f32[64,13]{0,1:T(8,128)S(1)}, f32[64,13]{0,1:T(8,128)}, u32[]{:S(2)}) copy-start(f32[64,13]{0,1:T(8,128)} %param.32) | copy-start | bytes 9988
  317.8 39.1 %copy-start.33 = (f32[64,1024]{1,0:T(8,128)S(1)}, f32[64,1024]{1,0:T(8,128)}, u32[]{:S(2)}) copy-start(f32[64,1024]{1,0:T(8,128)} %param.22) | copy-start | bytes 786436
  317.8 39.1 %copy-start.42 = (f32[64,1024]{1,0:T(8,128)S(1)}, f32[64,1024]{1,0:T(8,128)}, u32[]{:S(2)}) copy-start(f32[64,1024]{1,0:T(8,128)} %param.24) | copy-start | bytes 786436
  317.8 39.1 %copy-start.43 = (f32[64,1024]{1,0:T(8,128)S(1)}, f32[64,1024]{1,0:T(8,128)}, u32[]{:S(2)}) copy-start(f32[64,1024]{1,0:T(8,128)} %param.23) | copy-start | bytes 786436
  317.8 5.2 %copy-start.3 = (bf16[16,32,1024]{2,1,0:T(8,128)(2,1)S(1)}, bf16[16,32,1024]{2,1,0:T(8,128)(2,1)}, u32[]{:S(2)}) copy-start(bf16[16,32,1024]{2,1,0:T(8,128)(2,1)} %copy-done.2) | copy-start | bytes 3145732
  355.1 3.7 copy-start.39
  364.7 3.3 copy-start.18
  364.7 3.3 copy-start.19
  364.7 3.3 copy-start.26
  364.7 3.3 copy-start.27
  368.0 2.3 copy-start.34
  368.0 3.0 copy-start.35
  368.0 3.1 copy-start.40
  (20 other events, 32.1 us)
